TPU v7x, 32 devices: a whole 2x2x4 slice. The times are simulated.
32 devices in a mesh: chan: 16 (over z, x, core), rows: 2 (over y).
Axes of the slice: x: 2, y: 2, z: 4, core: 2. Of those that a mesh axis runs over, the one named last changes fastest.
Arguments:
- inputs: bfloat16 [1, 2, 256, 2048], P(None, 'rows', None, 'chan'), may hold values from -6 to 6
- weights: bfloat16 [3, 3, 2048, 2048], P(None, None, 'chan'), may hold values from -0.0625 to 0.0625
- cotangent: bfloat16 [1, 2, 256, 2048], P(None, 'rows', None, 'chan'), may hold values from -6 to 6
Outputs:
- outputs: bfloat16 [1, 2, 256, 2048], P(None, 'rows', None, 'chan')
- input_grad: bfloat16 [1, 2, 256, 2048], P(None, 'rows', None, 'chan')
- weight_grad: float32 [3, 3, 2048, 2048], P(None, None, 'chan', 'rows')
All inputs are finite; a program needn't handle non-finite values.
Results may differ from a plain program's by a relative error of at most 0.001.
Values may be sent and summed in bfloat16 or wider, within the bound.
A program may use at most 128 MiB of HBM per device.

v0:
```python
import jax
import jax.numpy as jnp
from jax import lax
from jax.sharding import PartitionSpec as P


def taps_of(padded, height, breadth):
    return [
        padded[:, ky : ky + height, kx : kx + breadth, :].reshape(-1, padded.shape[3])
        for ky in range(3)
        for kx in range(3)
    ]


def rim(array):
    return jnp.pad(array, ((0, 0), (1, 1), (1, 1), (0, 0)))


def on_device(inputs, weights, cotangent):
    batches, height, breadth, local_ch = inputs.shape
    channels = weights.shape[3]
    groups = lax.axis_size("rows")
    row = lax.axis_index("rows")
    share = channels // groups
    total_pixels = batches * height * groups * breadth

    def around(padded):
        return lax.dynamic_slice_in_dim(padded, row * height, height + 2, axis=1)

    in_padded = rim(lax.all_gather(inputs, "rows", axis=1, tiled=True))
    cot_all = lax.all_gather(
        lax.all_gather(cotangent, "chan", axis=3, tiled=True), "rows", axis=1, tiled=True
    )
    columns = jnp.concatenate(taps_of(around(in_padded), height, breadth), axis=1)
    conv_out = lax.psum_scatter(
        lax.dot_general(
            weights.reshape(9 * local_ch, channels),
            columns,
            (((0,), (1,)), ((), ())),
            preferred_element_type=jnp.float32,
        ),
        "chan",
        scatter_dimension=0,
        tiled=True,
    )
    outputs = conv_out.T.reshape(batches, height, breadth, local_ch).astype(jnp.bfloat16)
    grad_taps = taps_of(around(rim(cot_all)), height, breadth)
    data_sum = 0.0
    for tap in range(9):
        data_sum += lax.dot_general(
            grad_taps[8 - tap],
            weights[tap // 3, tap % 3],
            (((1,), (1,)), ((), ())),
            preferred_element_type=jnp.float32,
        )
    input_grad = data_sum.reshape(batches, height, breadth, local_ch).astype(jnp.bfloat16)
    all_columns = jnp.concatenate(taps_of(in_padded, height * groups, breadth), axis=1)
    mine = lax.dynamic_slice_in_dim(cot_all, row * share, share, axis=3)
    update = lax.dot_general(
        all_columns,
        mine.reshape(total_pixels, share),
        (((0,), (0,)), ((), ())),
        preferred_element_type=jnp.float32,
    )
    weight_grad = (update / jnp.sqrt(jnp.float32(total_pixels))).reshape(3, 3, local_ch, share)
    return (outputs, input_grad, weight_grad)


def solution(mesh):
    in_specs = (
        P(None, "rows", None, "chan"),
        P(None, None, "chan", None),
        P(None, "rows", None, "chan"),
    )
    out_specs = (
        P(None, "rows", None, "chan"),
        P(None, "rows", None, "chan"),
        P(None, None, "chan", "rows"),
    )
    return jax.shard_map(
        on_device, mesh=mesh, in_specs=in_specs, out_specs=out_specs, check_vma=False
    )
```

profile of v0, /device:TPU:0, one launch (start us, length us, event | category | flops | bytes accessed | tf_op | source)
XLA Modules:
  0.0 166.6 jit_solution(7292825136925069916)
XLA Ops:
  7.2 0.0 all-gather.3.cloned.1.call-start
  7.2 0.7 all-gather.3.cloned.1.call-update
  7.9 0.0 reduce-scatter.2.cloned.1.call-start
  7.9 6.1 %all_gather.9 = bf16[1,2,256,128]{3,2,0,1:T(8,128)(2,1)S(1)} all-gather(bf16[1,1,256,128]{3,2,0,1:T(8,128)(2,1)} %bitcast.139), channel_id=1, replica_groups=mesh['chan'=16,'rows'=2] {'rows'}, dimensions={1}, use_global_device_ids=true | all-gather | bytes 196608 | tf_op jit(solution)/shard_map/all_gather | solution.py:30
  14.1 0.1 fusion.39
  14.4 0.1 fusion.41
  14.5 5.2 %convolution_bitcast_fusion = f32[2048,256]{0,1:T(8,128)} fusion(bf16[256,1152]{1,0:T(8,128)(2,1)S(1)} %fusion.41, bf16[1152,2048]{1,0:T(8,128)(2,1)} %bitcast.126), kind=kOutput, calls=%fused_computation.10 | convolution fusion | flops 1207959552 | bytes 7405568 | tf_op jit(solution)/shard_map/dot_general | solution.py:36
  19.7 0.0 reduce-scatter.2.cloned.1.call-update
  19.7 0.0 all-gather.5.cloned.1.call-start
  19.8 29.9 %all-gather.3.cloned.1.call-done = bf16[1,1,256,2048]{3,2,0,1:T(8,128)(2,1)} async-done(((bf16[1,1,256,128]{3,2,0,1:T(8,128)(2,1)}), bf16[1,1,256,2048]{3,2,0,1:T(8,128)(2,1)}) %all-gather.3.cloned.1.call-update) | async-done | bytes 1048592 | tf_op jit(solution)/shard_map/all_gather | solution.py:32
  49.7 0.0 all-gather.5.cloned.1.call-update
  49.7 0.1 pad_slice_fusion
  50.2 64.8 %reduce-scatter.2.cloned.1.call-done = f32[128,256]{0,1:T(8,128)} async-done(((f32[2048,256]{0,1:T(8,128)}), f32[128,256]{0,1:T(8,128)}) %reduce-scatter.2.cloned.1.call-update) | async-done | bytes 131088 | tf_op jit(solution)/shard_map/reduce_scatter | solution.py:35
  115.0 1.5 convert_bitcast_fusion
  116.6 32.3 %all-gather.5.cloned.1.call-done = bf16[1,2,256,2048]{3,2,0,1:T(8,128)(2,1)} async-done(((bf16[1,1,256,2048]{3,2,0,1:T(8,128)(2,1)}), bf16[1,2,256,2048]{3,2,0,1:T(8,128)(2,1)}) %all-gather.5.cloned.1.call-update) | async-done | bytes 2097168 | tf_op jit(solution)/shard_map/all_gather | solution.py:31
  148.9 0.0 slice-start
  148.9 1.4 constant_dynamic-slice_fusion
  150.3 0.0 copy-start
  150.3 0.0 slice-start.1
  150.3 3.6 %convolution_multiply_fusion = f32[1152,1024]{1,0:T(8,128)} fusion(bf16[512,1152]{1,0:T(8,128)(2,1)S(1)} %constant_dynamic-update-slice_fusion, bf16[512,1024]{1,0:T(8,128)(2,1)S(1)} %bitcast.129), kind=kOutput, calls=%fused_computation.9 | convolution fusion | flops 1209139200 | bytes 6946816 | tf_op jit(solution)/shard_map/dot_general | solution.py:59
  154.0 0.0 copy-done
  154.0 1.5 fusion.19
  155.5 0.0 slice-done
  155.5 0.0 slice-done.1
  155.5 0.5 convolution_add_fusion.7
  156.0 0.5 convolution_add_fusion.6
  156.5 0.5 convolution_add_fusion.5
  157.0 0.4 convolution_add_fusion.4
  157.5 0.5 convolution_add_fusion.3
  158.0 0.5 convolution_add_fusion.2
  158.5 0.4 convolution_add_fusion.1
  158.9 1.1 fusion.1
  (18 shorter events, 0.5 us)
Async XLA Ops:
  7.2 42.5 %all-gather.3.cloned.1.call-start = ((), (), s32[]{:S(2)}) async-start(), calls=%async_computation.2 | async-start | bytes 1114112 | tf_op jit(solution)/shard_map/all_gather | solution.py:32
  7.9 107.1 %reduce-scatter.2.cloned.1.call-start = ((), (), s32[]{:S(2)}) async-start(), calls=%async_computation.1 | async-start | bytes 2228224 | tf_op jit(solution)/shard_map/reduce_scatter | solution.py:35
  19.7 129.1 %all-gather.5.cloned.1.call-start = ((), (), s32[]{:S(2)}) async-start(), calls=%async_computation.3 | async-start | bytes 3145728 | tf_op jit(solution)/shard_map/all_gather | solution.py:31
  148.9 6.6 %slice-start = ((s8[4718592]{0:T(1024)(128)(4,1)}), s8[4194304]{0:T(1024)(128)(4,1)S(1)}, s32[]{:S(2)}) async-start(s8[4718592]{0:T(1024)(128)(4,1)} %bitcast.127), calls=%async_computation.4 | async-start | bytes 8388608
  150.3 3.7 %copy-start = (bf16[1,2,256,2048]{3,2,0,1:T(8,128)(2,1)S(1)}, bf16[1,2,256,2048]{3,2,0,1:T(8,128)(2,1)}, u32[]{:S(2)}) copy-start(bf16[1,2,256,2048]{3,2,0,1:T(8,128)(2,1)} %all-gather.5.cloned.1.call-done) | copy-start | bytes 6291460
  150.3 5.2 %slice-start.1 = ((s8[4718592]{0:T(1024)(128)(4,1)}), s8[524288]{0:T(1024)(128)(4,1)S(1)}, s32[]{:S(2)}) async-start(s8[4718592]{0:T(1024)(128)(4,1)} %bitcast.127), calls=%async_computation.5 | async-start | bytes 1048576
Sparse Core Ops, SparseCore 0:
  10.2 39.4 all-gather.2
  54.0 60.9 reduce-scatter.1
  116.7 32.1 all-gather.4
where the time goes:
time: 167 us
  waiting for transfers between devices  128 us (77%)
  matrix products  14.9 us (9%)
  between operations  14 us (8%)
  blocking collectives  6.14 us (4%)
  local copies, waits for them, and re-layouts  2.23 us (1%)
    reduce_scatter x1, waiting for transfers between devices, on_device(): lax.psum_scatter(lax.dot_general(weights.reshape(9 * local_ch, channels),...  64.8 us
    all_gather x1, waiting for transfers between devices, on_device(): lax.all_gather(lax.all_gather(cotangent, 'chan', axis=3, tiled=True), 'ro...  32.3 us
    all_gather x1, waiting for transfers between devices, on_device(): lax.all_gather(cotangent, 'chan', axis=3, tiled=True)  29.9 us
    all_gather x1, blocking collectives, on_device(): in_padded = rim(lax.all_gather(inputs, 'rows', axis=1, tiled=True))  6.14 us
    dot_general x9, matrix products, on_device(): lax.dot_general(grad_taps[8 - tap], weights[tap // 3, tap % 3], (((1,), (...  6.04 us
    dot_general x1, matrix products, on_device(): lax.dot_general(weights.reshape(9 * local_ch, channels), columns, (((0,),...  5.23 us
    dot_general x1, matrix products, on_device(): lax.dot_general(all_columns, mine.reshape(total_pixels, share), (((0,), (...  3.62 us
  transfers between devices with their start and end apart: 3, of which 3 were waited for; matrix products, arithmetic and copies ran while one was open for 5% of the time, Pallas kernels for 0%

commit v1 on v0

--- a/solution.py
+++ b/solution.py
@@ -28,9 +28,16 @@
         return lax.dynamic_slice_in_dim(padded, row * height, height + 2, axis=1)
 
     in_padded = rim(lax.all_gather(inputs, "rows", axis=1, tiled=True))
-    cot_all = lax.all_gather(
-        lax.all_gather(cotangent, "chan", axis=3, tiled=True), "rows", axis=1, tiled=True
-    )
+    x = lax.all_gather(cotangent, "chan", axis=3, tiled=True)
+    ways, here, step = (lax.axis_size("rows"), lax.axis_index("rows"), x.shape[1])
+    line, have = (x, 1)
+    while have < ways:
+        line = jnp.concatenate(
+            [line, lax.ppermute(line, "rows", [(d, (d - have) % ways) for d in range(ways)])],
+            axis=1,
+        )
+        have = 2 * have
+    cot_all = jnp.roll(line, here * step, axis=1)
     columns = jnp.concatenate(taps_of(around(in_padded), height, breadth), axis=1)
     conv_out = lax.psum_scatter(
         lax.dot_general(

time: 167 us -> 123 us (0.74)
  waiting for transfers between devices: 128 us -> 83.4 us
    reduce_scatter x1, waiting for transfers between devices: 64.8 us -> 29.3 us  [on_device(): lax.psum_scatter(lax.dot_general(weights.reshape(9 * local_ch, channels),...]
    all_gather x2 -> x1, waiting for transfers between devices: 62.2 us -> 29.7 us  [on_device(): x = lax.all_gather(cotangent, 'chan', axis=3, tiled=True)]
    ppermute x0 -> x1, waiting for transfers between devices: none -> 23.8 us  [on_device(): lax.ppermute(line, 'rows', [(d, (d - have) % ways) for d in range(ways)])]
  transfers between devices with their start and end apart: 3 -> 3, of which waited for: 3 -> 3; matrix products, arithmetic and copies ran while one was open for 5% -> 13% of each run, Pallas kernels for 0% -> 0%
where the time goes in v1:
time: 123 us
  waiting for transfers between devices  83.4 us (68%)
  between operations  14.3 us (12%)
  matrix products  13.9 us (11%)
  blocking collectives  6.14 us (5%)
  local copies, waits for them, and re-layouts  2.05 us (2%)
  other arithmetic  1.54 us (1%)
  starting transfers between devices  1.45 us (1%)
    all_gather x1, waiting for transfers between devices, on_device(): x = lax.all_gather(cotangent, 'chan', axis=3, tiled=True)  29.7 us
    reduce_scatter x1, waiting for transfers between devices, on_device(): lax.psum_scatter(lax.dot_general(weights.reshape(9 * local_ch, channels),...  29.3 us
    ppermute x1, waiting for transfers between devices, on_device(): lax.ppermute(line, 'rows', [(d, (d - have) % ways) for d in range(ways)])  23.8 us
    all_gather x1, blocking collectives, on_device(): in_padded = rim(lax.all_gather(inputs, 'rows', axis=1, tiled=True))  6.14 us
    dot_general x1, matrix products, on_device(): lax.dot_general(weights.reshape(9 * local_ch, channels), columns, (((0,),...  5.25 us
    dot_general x9, matrix products, on_device(): lax.dot_general(grad_taps[8 - tap], weights[tap // 3, tap % 3], (((1,), (...  5.02 us
    dot_general x1, matrix products, on_device(): lax.dot_general(all_columns, mine.reshape(total_pixels, share), (((0,), (...  3.62 us
  transfers between devices with their start and end apart: 3, of which 3 were waited for; matrix products, arithmetic and copies ran while one was open for 13% of the time, Pallas kernels for 0%

profile of v1, /device:TPU:0, one launch (start us, length us, event | category | flops | bytes accessed | tf_op | source)
XLA Modules:
  0.0 122.8 jit_solution(1348946592987394194)
XLA Ops:
  7.2 0.0 all-gather.2.cloned.1.call-start
  7.2 0.7 all-gather.2.cloned.1.call-update
  7.9 0.0 reduce-scatter.2.cloned.1.call-start
  7.9 6.1 %all_gather.6 = bf16[1,2,256,128]{3,2,0,1:T(8,128)(2,1)S(1)} all-gather(bf16[1,1,256,128]{3,2,0,1:T(8,128)(2,1)} %bitcast.138), channel_id=1, replica_groups=mesh['chan'=16,'rows'=2] {'rows'}, dimensions={1}, use_global_device_ids=true | all-gather | bytes 196608 | tf_op jit(solution)/shard_map/all_gather | solution.py:30
  14.1 0.1 fusion.39
  14.4 0.1 fusion.41
  14.5 5.2 %convolution_bitcast_fusion = f32[2048,256]{0,1:T(8,128)} fusion(bf16[256,1152]{1,0:T(8,128)(2,1)S(1)} %fusion.41, bf16[1152,2048]{1,0:T(8,128)(2,1)} %bitcast.125), kind=kOutput, calls=%fused_computation.10 | convolution fusion | flops 1207959552 | bytes 7405568 | tf_op jit(solution)/shard_map/dot_general | solution.py:43
  19.7 0.0 reduce-scatter.2.cloned.1.call-update
  19.8 0.1 pad_slice_fusion
  20.0 29.7 %all-gather.2.cloned.1.call-done = bf16[1,1,256,2048]{3,2,1,0:T(8,128)(2,1)} async-done(((bf16[1,1,256,128]{3,2,1,0:T(8,128)(2,1)}), bf16[1,1,256,2048]{3,2,1,0:T(8,128)(2,1)}) %all-gather.2.cloned.1.call-update) | async-done | bytes 1048592 | tf_op jit(solution)/shard_map/all_gather | solution.py:31
  49.7 1.4 %collective-permute-start = (bf16[1,1,256,2048]{3,2,1,0:T(8,128)(2,1)}, bf16[1,1,256,2048]{3,2,1,0:T(8,128)(2,1)S(1)}, u32[]{:S(2)}, u32[]{:S(2)}) collective-permute-start(bf16[1,1,256,2048]{3,2,1,0:T(8,128)(2,1)} %all-gather.2.cloned.1.call-done), channel_id=1, source_target_pairs={{0,1},{1,0},{2,3},{3,2},{4,5},{5,4},{6,7},{7,6},{8,9},{9,8},{10,11... | collective-permute-start | bytes 3145736 | tf_op jit(solution)/shard_map/ppermute | solution.py:36
  51.4 0.0 slice-start
  51.4 0.1 constant_dynamic-update-slice_fusion.3
  51.5 23.8 %collective-permute-done = bf16[1,1,256,2048]{3,2,1,0:T(8,128)(2,1)S(1)} collective-permute-done((bf16[1,1,256,2048]{3,2,1,0:T(8,128)(2,1)}, bf16[1,1,256,2048]{3,2,1,0:T(8,128)(2,1)S(1)}, u32[]{:S(2)}, u32[]{:S(2)}) %collective-permute-start) | collective-permute-done | bytes 1048608 | tf_op jit(solution)/shard_map/ppermute | solution.py:36
  75.2 0.1 constant_dynamic-update-slice_fusion.2
  75.3 0.1 constant_dynamic-update-slice_fusion.1
  75.4 0.0 slice-start.1
  75.4 0.1 constant_dynamic-update-slice_fusion
  75.5 0.7 constant_dynamic-slice_fusion
  76.2 0.2 constant_dynamic-slice_fusion.1
  76.5 0.4 fusion.19
  77.0 0.5 convolution_add_fusion.7
  77.5 0.5 convolution_add_fusion.6
  78.0 0.5 convolution_add_fusion.5
  78.5 0.4 convolution_add_fusion.4
  79.0 0.5 convolution_add_fusion.3
  79.5 0.5 convolution_add_fusion.2
  80.0 0.4 convolution_add_fusion.1
  80.4 1.1 fusion.1
  81.6 3.6 %convolution_multiply_fusion = f32[1152,1024]{1,0:T(8,128)} fusion(bf16[512,1152]{1,0:T(8,128)(2,1)S(1)} %constant_dynamic-update-slice_fusion.4, bf16[512,1024]{1,0:T(8,128)(2,1)S(1)} %bitcast.128), kind=kOutput, calls=%fused_computation.9 | convolution fusion | flops 1209139200 | bytes 6946816 | tf_op jit(solution)/shard_map/dot_general | solution.py:66
  85.2 29.3 %reduce-scatter.2.cloned.1.call-done = f32[128,256]{0,1:T(8,128)} async-done(((f32[2048,256]{0,1:T(8,128)}), f32[128,256]{0,1:T(8,128)}) %reduce-scatter.2.cloned.1.call-update) | async-done | bytes 131088 | tf_op jit(solution)/shard_map/reduce_scatter | solution.py:42
  114.5 1.5 %convert_bitcast_fusion = bf16[1,1,256,128]{3,2,1,0:T(8,128)(2,1)} fusion(f32[128,256]{0,1:T(8,128)} %reduce-scatter.2.cloned.1.call-done), kind=kLoop, calls=%fused_computation.78 | loop fusion | flops 32768 | bytes 196608 | tf_op jit(solution)/shard_map/convert_element_type | solution.py:53
  (22 shorter events, 0.5 us)
Async XLA Ops:
  7.2 42.5 %all-gather.2.cloned.1.call-start = ((), (), s32[]{:S(2)}) async-start(), calls=%async_computation.2 | async-start | bytes 1114112 | tf_op jit(solution)/shard_map/all_gather | solution.py:31
  7.9 106.6 %reduce-scatter.2.cloned.1.call-start = ((), (), s32[]{:S(2)}) async-start(), calls=%async_computation.1 | async-start | bytes 2228224 | tf_op jit(solution)/shard_map/reduce_scatter | solution.py:42
  49.7 1.7 %copy-start = (bf16[1,1,256,2048]{3,2,1,0:T(8,128)(2,1)S(1)}, bf16[1,1,256,2048]{3,2,1,0:T(8,128)(2,1)}, u32[]{:S(2)}) copy-start(bf16[1,1,256,2048]{3,2,1,0:T(8,128)(2,1)} %all-gather.2.cloned.1.call-done) | copy-start | bytes 3145732
  49.7 25.5 %collective-permute-start = (bf16[1,1,256,2048]{3,2,1,0:T(8,128)(2,1)}, bf16[1,1,256,2048]{3,2,1,0:T(8,128)(2,1)S(1)}, u32[]{:S(2)}, u32[]{:S(2)}) collective-permute-start(bf16[1,1,256,2048]{3,2,1,0:T(8,128)(2,1)} %all-gather.2.cloned.1.call-done), channel_id=1, source_target_pairs={{0,1},{1,0},{2,3},{3,2},{4,5},{5,4},{6,7},{7,6},{8,9},{9,8},{10,11... | collective-permute-start | bytes 3145736 | tf_op jit(solution)/shard_map/ppermute | solution.py:36
  51.4 25.1 %slice-start = ((s8[4718592]{0:T(1024)(128)(4,1)}), s8[4194304]{0:T(1024)(128)(4,1)S(1)}, s32[]{:S(2)}) async-start(s8[4718592]{0:T(1024)(128)(4,1)} %bitcast.126), calls=%async_computation.3 | async-start | bytes 8388608
  75.4 1.1 slice-start.1
Sparse Core Ops, SparseCore 0:
  10.2 39.4 all-gather.1
  53.4 60.9 reduce-scatter.1
